TPU v7x, 256 devices: a whole 4x4x8 slice. The times are simulated.
256 devices in a mesh: seq: 64 (over y, z, core), chan: 4 (over x).
Axes of the slice: x: 4, y: 4, z: 8, core: 2. Of those that a mesh axis runs over, the one named last changes fastest.
Arguments:
- inputs: bfloat16 [32768, 1536], P('seq', 'chan'), may hold values from -16 to 16
- conv_weight: bfloat16 [1, 3, 1536, 1536], P(None, None, None, 'chan'), may hold values from -0.09375 to 0.09375
- head_weight: bfloat16 [1536, 4096], P(None, 'chan'), may hold values from -0.15625 to 0.15625
- head_cot: bfloat16 [32768, 4096], P('seq', 'chan'), may hold values from -6 to 6
- exon_blocks: int32 [512, 8], P('seq'), may hold values from 0 to 255
Outputs:
- tracks: bfloat16 [32768, 4096], P('seq', 'chan')
- coverage: float32 [512, 4096], P('seq', 'chan')
- input_grad: bfloat16 [32768, 1536], P('seq', 'chan')
- kernel_gradient: float32 [1, 3, 1536, 1536], P(None, None, 'seq', 'chan')
All inputs are finite; a program needn't handle non-finite values.
Results may differ from a plain program's by a relative error of at most 0.0059.
Values may be sent and summed in bfloat16 or wider, within the bound.
No kernel may reach another device: no remote copies, remote signals or barrier semaphores. Data moves between devices by JAX's collectives and lax.ppermute only.
A program may use at most 64 MiB of HBM per device.

v0:
```python
import jax
import jax.numpy as jnp
from jax import lax
from jax.sharding import PartitionSpec as P

BLOCK = 128
EXONS = 8


def shifted(value, axis, steps):
    count = lax.axis_size(axis)
    leading, last = (max(0, -steps), min(count, count - steps))
    return lax.ppermute(value, axis, [(source, source + steps) for source in range(leading, last)])


def activation_slope(point, cotan):
    _, back = jax.vjp(jax.nn.gelu, point)
    return back(cotan)[0]


def tap_input(values, steps):
    return shifted(values, "seq", steps)


def tap_grad(values, steps):
    return shifted(values, "seq", steps)


def times_t(left, right):
    return lax.dot_general(
        left, right, (((1,), (1,)), ((), ())), preferred_element_type=jnp.float32
    )


def inner_rows(left, right):
    return lax.dot_general(
        left, right, (((0,), (0,)), ((), ())), preferred_element_type=jnp.float32
    )


def shards(inputs, conv_weight, head_weight, head_cot, exon_blocks):
    rows = inputs.shape[0]
    state = inputs
    layer_number = 0
    steps = 2 * 2**layer_number
    acted = jax.nn.gelu(state.astype(jnp.float32)).astype(jnp.bfloat16)
    lower = tap_input(acted, steps)
    upper = tap_input(acted, -steps)
    whole = lax.all_gather(acted, "chan", axis=1, tiled=True)
    whole_low = lax.all_gather(lower, "chan", axis=1, tiled=True)
    whole_up = lax.all_gather(upper, "chan", axis=1, tiled=True)
    mixed = jnp.dot(whole_low, conv_weight[layer_number, 0], preferred_element_type=jnp.float32)
    mixed = mixed + jnp.dot(whole, conv_weight[layer_number, 1], preferred_element_type=jnp.float32)
    mixed = mixed + jnp.dot(
        whole_up, conv_weight[layer_number, 2], preferred_element_type=jnp.float32
    )
    saved = [(state, whole, steps)]
    state = (state.astype(jnp.float32) + mixed).astype(jnp.bfloat16)
    full_state = lax.all_gather(state, "chan", axis=1, tiled=True)
    logits = jnp.dot(full_state, head_weight, preferred_element_type=jnp.float32)
    tracks = jax.nn.softplus(logits).astype(jnp.bfloat16)
    head_term = (head_cot.astype(jnp.float32) * jax.nn.sigmoid(logits)).astype(jnp.bfloat16)
    grad = lax.psum_scatter(
        times_t(head_term, head_weight), "chan", scatter_dimension=1, tiled=True
    )
    grads = []
    for layer_number in reversed(range(conv_weight.shape[0])):
        before, whole, steps = saved[layer_number]
        grad_low = grad.astype(jnp.bfloat16)
        later = tap_grad(grad_low, -steps)
        earlier = tap_grad(grad_low, steps)
        partial_value = times_t(later, conv_weight[layer_number, 0])
        partial_value = partial_value + times_t(grad_low, conv_weight[layer_number, 1])
        partial_value = partial_value + times_t(earlier, conv_weight[layer_number, 2])
        back_u = lax.psum_scatter(partial_value, "chan", scatter_dimension=1, tiled=True)
        kernel = jnp.stack(
            [inner_rows(whole, later), inner_rows(whole, grad_low), inner_rows(whole, earlier)]
        )
        grads.append(lax.psum_scatter(kernel, "seq", scatter_dimension=1, tiled=True))
        grad = grad + activation_slope(before.astype(jnp.float32), back_u)
    kernel_gradient = jnp.stack(grads[::-1])
    resident_blocks = rows // BLOCK
    block_partial_sums = (
        tracks.astype(jnp.float32).reshape(resident_blocks, BLOCK, tracks.shape[1]).sum(axis=1)
    )
    scale = jnp.sqrt(jnp.float32(EXONS * BLOCK))
    all_blocks = lax.all_gather(block_partial_sums, "seq", axis=0, tiled=True)
    labels = jnp.arange(all_blocks.shape[0], dtype=jnp.int32)
    counts = jnp.sum((exon_blocks[:, :, None] == labels[None, None, :]).astype(jnp.float32), axis=1)
    coverage = jnp.dot(counts, all_blocks, precision=lax.Precision.HIGHEST) / scale
    return (tracks, coverage, grad.astype(jnp.bfloat16), kernel_gradient)


def solution(mesh):
    return jax.shard_map(
        shards,
        mesh=mesh,
        in_specs=(
            P("seq", "chan"),
            P(None, None, None, "chan"),
            P(None, "chan"),
            P("seq", "chan"),
            P("seq", None),
        ),
        out_specs=(
            P("seq", "chan"),
            P("seq", "chan"),
            P("seq", "chan"),
            P(None, None, "seq", "chan"),
        ),
        check_vma=False,
    )
```

profile of v0, /device:TPU:2, one launch (start us, length us, event | category | flops | bytes accessed | tf_op | source)
XLA Modules:
  0.0 468.9 jit_solution(14514463337364591084)
XLA Ops:
  7.2 0.0 all-gather.9.cloned.1.call-start
  7.2 2.2 fusion.30
  9.4 0.0 all-gather.9.cloned.1.call-update
  9.4 0.0 all-gather.11.cloned.1.call-start
  9.5 1.3 collective-permute-start.1
  10.8 11.8 %collective-permute-done.1 = bf16[512,384]{1,0:T(8,128)(2,1)S(1)} collective-permute-done((bf16[512,384]{1,0:T(8,128)(2,1)}, bf16[512,384]{1,0:T(8,128)(2,1)S(1)}, u32[]{:S(2)}, u32[]{:S(2)}) %collective-permute-start.1) | collective-permute-done | bytes 393248 | tf_op jit(solution)/shard_map/ppermute | solution.py:13
  22.6 0.7 copy-done.8
  23.4 0.0 all-gather.7.cloned.1.call-start
  23.4 3.8 collective-permute-start
  27.3 8.0 %collective-permute-done = bf16[512,384]{1,0:T(8,128)(2,1)S(1)} collective-permute-done((bf16[512,384]{1,0:T(8,128)(2,1)}, bf16[512,384]{1,0:T(8,128)(2,1)S(1)}, u32[]{:S(2)}, u32[]{:S(2)}) %collective-permute-start) | collective-permute-done | bytes 393248 | tf_op jit(solution)/shard_map/ppermute | solution.py:13
  35.3 0.7 copy-done.9
  36.0 0.0 all-gather.13.cloned.1.call-start
  36.1 5.5 %all-gather.9.cloned.1.call-done = bf16[512,1536]{1,0:T(8,128)(2,1)} async-done(((bf16[512,384]{1,0:T(8,128)(2,1)}), bf16[512,1536]{1,0:T(8,128)(2,1)}) %all-gather.9.cloned.1.call-update) | async-done | bytes 1572880 | tf_op jit(solution)/shard_map/all_gather | solution.py:49
  41.5 3.6 fusion.10
  45.2 27.9 %all-gather.11.cloned.1.call-done = bf16[512,1536]{1,0:T(8,128)(2,1)} async-done(((bf16[512,384]{1,0:T(8,128)(2,1)}), bf16[512,1536]{1,0:T(8,128)(2,1)}) %all-gather.11.cloned.1.call-update) | async-done | bytes 1572880 | tf_op jit(solution)/shard_map/all_gather | solution.py:51
  73.1 3.6 fusion.6
  76.7 27.4 %all-gather.7.cloned.1.call-done = bf16[512,1536]{1,0:T(8,128)(2,1)} async-done(((bf16[512,384]{1,0:T(8,128)(2,1)}), bf16[512,1536]{1,0:T(8,128)(2,1)}) %all-gather.7.cloned.1.call-update) | async-done | bytes 1572880 | tf_op jit(solution)/shard_map/all_gather | solution.py:50
  104.1 3.9 fusion.3
  108.1 0.0 reduce-scatter.4.cloned.1.call-start
  108.1 29.2 %all-gather.13.cloned.1.call-done = bf16[512,1536]{1,0:T(8,128)(2,1)} async-done(((bf16[512,384]{1,0:T(8,128)(2,1)}), bf16[512,1536]{1,0:T(8,128)(2,1)}) %all-gather.13.cloned.1.call-update) | async-done | bytes 1572880 | tf_op jit(solution)/shard_map/all_gather | solution.py:59
  137.4 5.8 %convert_reduce_fusion = (f32[4,1024]{1,0:T(4,128)}, bf16[512,1024]{1,0:T(8,128)(2,1)}, f32[512,1024]{1,0:T(8,128)S(1)}) fusion(bf16[512,1536]{1,0:T(8,128)(2,1)} %all-gather.13.cloned.1.call-done, bf16[1536,1024]{1,0:T(8,128)(2,1)S(1)} %copy-done), kind=kOutput, calls=%fused_computation.8 | convolution fusion | flops 1615327232 | bytes 7880704 | tf_op jit(solution)/shard_map/dot_general | solution.py:60
  143.2 3.5 fusion.15
  146.7 0.0 all-gather.15.cloned.1.call-start
  146.8 0.5 all-gather.15.cloned.1.call-update
  147.3 0.0 reduce-scatter.6.cloned.1.call-start
  147.3 40.1 %reduce-scatter.4.cloned.1.call-done = f32[512,384]{1,0:T(8,128)} async-done(((f32[512,1536]{1,0:T(8,128)}), f32[512,384]{1,0:T(8,128)}) %reduce-scatter.4.cloned.1.call-update) | async-done | bytes 786448 | tf_op jit(solution)/shard_map/reduce_scatter | solution.py:63
  187.4 1.2 convert_element_type.37
  188.6 3.7 collective-permute-start.3
  192.4 1.3 collective-permute-start.2
  193.7 2.3 fusion.8
  196.0 4.8 %collective-permute-done.3 = bf16[512,384]{1,0:T(8,128)(2,1)S(1)} collective-permute-done((bf16[512,384]{1,0:T(8,128)(2,1)S(1)}, bf16[512,384]{1,0:T(8,128)(2,1)S(1)}, u32[]{:S(2)}, u32[]{:S(2)}) %collective-permute-start.3) | collective-permute-done | bytes 393248 | tf_op jit(solution)/shard_map/ppermute | solution.py:13
  200.8 1.0 fusion.4
  201.8 3.1 collective-permute-done.2
  204.9 0.7 copy-done.4
  205.6 2.7 fusion
  208.4 0.2 reduce-scatter.8.cloned.1.call-start
  208.6 2.6 convolution_bitcast_fusion.1
  211.3 1.0 convolution_bitcast_fusion
  212.3 1.0 convolution_bitcast_fusion.2
  213.3 3.3 pad_maximum_fusion
  216.7 0.7 copy-done.10
  217.4 0.1 convert_reduce_fusion.1
  217.4 50.6 %all-gather.15.cloned.1.call-done = f32[64,4,1024]{2,1,0:T(4,128)} async-done(((f32[1,4,1024]{2,1,0:T(4,128)}), f32[64,4,1024]{2,1,0:T(4,128)}) %all-gather.15.cloned.1.call-update) | async-done | bytes 1048592 | tf_op jit(solution)/shard_map/all_gather | solution.py:87
  268.0 2.6 reshape.20
  270.6 2.4 convolution_multiply_fusion
  273.1 34.8 %reduce-scatter.6.cloned.1.call-done = f32[512,384]{1,0:T(8,128)} async-done(((f32[512,1536]{1,0:T(8,128)}), f32[512,384]{1,0:T(8,128)}) %reduce-scatter.6.cloned.1.call-update) | async-done | bytes 786448 | tf_op jit(solution)/shard_map/reduce_scatter | solution.py:75
  307.9 2.7 fusion.26
  310.6 151.5 %reduce-scatter.8.cloned.1.call-done = f32[3,24,384]{2,1,0:T(8,128)} async-done(((f32[3,1536,384]{2,1,0:T(8,128)}), f32[3,24,384]{2,1,0:T(8,128)}) %reduce-scatter.8.cloned.1.call-update) | async-done | bytes 110608 | tf_op jit(solution)/shard_map/reduce_scatter | solution.py:79
  (28 shorter events, 0.2 us)
Async XLA Ops:
  7.2 130.2 %copy-start = (bf16[1536,1024]{1,0:T(8,128)(2,1)S(1)}, bf16[1536,1024]{1,0:T(8,128)(2,1)}, u32[]{:S(2)}) copy-start(bf16[1536,1024]{1,0:T(8,128)(2,1)} %param.7) | copy-start | bytes 9437188
  7.2 34.4 %all-gather.9.cloned.1.call-start = ((), (), s32[]{:S(2)}) async-start(), calls=%async_computation.4 | async-start | bytes 1966080 | tf_op jit(solution)/shard_map/all_gather | solution.py:49
  9.4 63.7 %all-gather.11.cloned.1.call-start = ((), (), s32[]{:S(2)}) async-start(), calls=%async_computation.5 | async-start | bytes 1966080 | tf_op jit(solution)/shard_map/all_gather | solution.py:51
  9.5 13.1 %collective-permute-start.1 = (bf16[512,384]{1,0:T(8,128)(2,1)}, bf16[512,384]{1,0:T(8,128)(2,1)S(1)}, u32[]{:S(2)}, u32[]{:S(2)}) collective-permute-start(bf16[512,384]{1,0:T(8,128)(2,1)} %fusion.30), channel_id=1, source_target_pairs={{8,0},{12,4},{16,8},{20,12},{24,16},{28,20},{32,24},{36,28},{40,32... | collective-permute-start | bytes 1179656 | tf_op jit(solution)/shard_map/ppermute | solution.py:13
  22.6 0.7 copy-start.8
  23.4 80.7 %all-gather.7.cloned.1.call-start = ((), (), s32[]{:S(2)}) async-start(), calls=%async_computation.3 | async-start | bytes 1966080 | tf_op jit(solution)/shard_map/all_gather | solution.py:50
  23.4 11.8 %collective-permute-start = (bf16[512,384]{1,0:T(8,128)(2,1)}, bf16[512,384]{1,0:T(8,128)(2,1)S(1)}, u32[]{:S(2)}, u32[]{:S(2)}) collective-permute-start(bf16[512,384]{1,0:T(8,128)(2,1)} %fusion.30), channel_id=1, source_target_pairs={{0,8},{4,12},{8,16},{12,20},{16,24},{20,28},{24,32},{28,36},{32,40... | collective-permute-start | bytes 1179656 | tf_op jit(solution)/shard_map/ppermute | solution.py:13
  35.3 0.7 copy-start.9
  36.0 101.3 %all-gather.13.cloned.1.call-start = ((), (), s32[]{:S(2)}) async-start(), calls=%async_computation.6 | async-start | bytes 1966080 | tf_op jit(solution)/shard_map/all_gather | solution.py:59
  45.2 59.0 %copy-start.2 = (bf16[512,384]{1,0:T(8,128)(2,1)S(1)}, bf16[512,384]{1,0:T(8,128)(2,1)}, u32[]{:S(2)}) copy-start(bf16[512,384]{1,0:T(8,128)(2,1)} %param.5) | copy-start | bytes 1179652
  108.1 79.3 %reduce-scatter.4.cloned.1.call-start = ((), (), s32[]{:S(2)}) async-start(), calls=%async_computation.7 | async-start | bytes 3932160 | tf_op jit(solution)/shard_map/reduce_scatter | solution.py:63
  137.4 5.8 %copy-start.12 = (bf16[512,1024]{1,0:T(8,128)(2,1)S(1)}, bf16[512,1024]{1,0:T(8,128)(2,1)}, u32[]{:S(2)}) copy-start(bf16[512,1024]{1,0:T(8,128)(2,1)} %param.8) | copy-start | bytes 3145732
  146.7 121.3 %all-gather.15.cloned.1.call-start = ((), (), s32[]{:S(2)}) async-start(), calls=%async_computation.10 | async-start | bytes 1064960 | tf_op jit(solution)/shard_map/all_gather | solution.py:87
  147.3 160.6 %reduce-scatter.6.cloned.1.call-start = ((), (), s32[]{:S(2)}) async-start(), calls=%async_computation.8 | async-start | bytes 3932160 | tf_op jit(solution)/shard_map/reduce_scatter | solution.py:75
  188.6 7.4 %copy-start.3 = (bf16[512,384]{1,0:T(8,128)(2,1)}, bf16[512,384]{1,0:T(8,128)(2,1)S(1)}, u32[]{:S(2)}) copy-start(bf16[512,384]{1,0:T(8,128)(2,1)S(1)} %convert_element_type.37) | copy-start | bytes 1179652
  188.6 12.1 %copy-start.1 = (bf16[1,3,1536,384]{3,2,1,0:T(8,128)(2,1)S(1)}, bf16[1,3,1536,384]{3,2,1,0:T(8,128)(2,1)}, u32[]{:S(2)}) copy-start(bf16[1,3,1536,384]{3,2,1,0:T(8,128)(2,1)} %param.6) | copy-start | bytes 10616836
  188.6 12.1 %collective-permute-start.3 = (bf16[512,384]{1,0:T(8,128)(2,1)S(1)}, bf16[512,384]{1,0:T(8,128)(2,1)S(1)}, u32[]{:S(2)}, u32[]{:S(2)}) collective-permute-start(bf16[512,384]{1,0:T(8,128)(2,1)S(1)} %convert_element_type.37), channel_id=1, source_target_pairs={{0,8},{4,12},{8,16},{12,20},{16,24},{20,28},{24,32},{28,36},{32,40... | collective-permute-start | bytes 1179656 | tf_op jit(solution)/shard_map/ppermute | solution.py:13
  192.4 12.5 %collective-permute-start.2 = (bf16[512,384]{1,0:T(8,128)(2,1)S(1)}, bf16[512,384]{1,0:T(8,128)(2,1)S(1)}, u32[]{:S(2)}, u32[]{:S(2)}) collective-permute-start(bf16[512,384]{1,0:T(8,128)(2,1)S(1)} %convert_element_type.37), channel_id=1, source_target_pairs={{8,0},{12,4},{16,8},{20,12},{24,16},{28,20},{32,24},{36,28},{40,32... | collective-permute-start | bytes 1179656 | tf_op jit(solution)/shard_map/ppermute | solution.py:13
  200.8 1.0 copy-start.6
  204.9 0.7 copy-start.4
  208.4 253.7 %reduce-scatter.8.cloned.1.call-start = ((), (), s32[]{:S(2)}) async-start(), calls=%async_computation.9 | async-start | bytes 7188480 | tf_op jit(solution)/shard_map/reduce_scatter | solution.py:79
  208.6 2.7 copy-start.7
  208.6 2.6 copy-start.11
  211.3 1.0 copy-start.5
  216.7 0.7 copy-start.10
Sparse Core Ops, SparseCore 0:
  10.4 31.0 all-gather.8
  44.0 29.1 all-gather.10
  75.0 29.1 all-gather.6
  108.2 29.1 all-gather.12
  146.8 40.5 reduce-scatter.3
  190.6 77.3 all-gather.14
  270.6 37.2 reduce-scatter.5
  312.7 149.2 reduce-scatter.7
where the time goes:
time: 469 us
  waiting for transfers between devices  395 us (84%)
  matrix products  33.6 us (7%)
  between operations  14.3 us (3%)
  starting transfers between devices  10.7 us (2%)
  other arithmetic  9.47 us (2%)
  local copies, waits for them, and re-layouts  5.52 us (1%)
    reduce_scatter x1, waiting for transfers between devices, shards(): lax.psum_scatter(kernel, 'seq', scatter_dimension=1, tiled=True)  151 us
    all_gather x1, waiting for transfers between devices, shards(): all_blocks = lax.all_gather(block_partial_sums, 'seq', axis=0, tiled=True)  50.6 us
    reduce_scatter x1, waiting for transfers between devices, shards(): lax.psum_scatter(times_t(head_term, head_weight), 'chan', scatter_dimensi...  40.1 us
    reduce_scatter x1, waiting for transfers between devices, shards(): lax.psum_scatter(partial_value, 'chan', scatter_dimension=1, tiled=True)  34.8 us
    all_gather x1, waiting for transfers between devices, shards(): full_state = lax.all_gather(state, 'chan', axis=1, tiled=True)  29.2 us
    all_gather x1, waiting for transfers between devices, shards(): whole_up = lax.all_gather(upper, 'chan', axis=1, tiled=True)  27.9 us
    ppermute x4, waiting for transfers between devices, shifted(): lax.ppermute(value, axis, [(source, source + steps) for source in range(l...  27.7 us
    all_gather x1, waiting for transfers between devices, shards(): whole_low = lax.all_gather(lower, 'chan', axis=1, tiled=True)  27.4 us
  transfers between devices with their start and end apart: 12, of which 12 were waited for; matrix products, arithmetic and copies ran while one was open for 6% of the time, Pallas kernels for 0%

commit v1 on v0

--- a/solution.py
+++ b/solution.py
@@ -48,7 +48,9 @@
     upper = tap_input(acted, -steps)
     whole = lax.all_gather(acted, "chan", axis=1, tiled=True)
     whole_low = lax.all_gather(lower, "chan", axis=1, tiled=True)
-    whole_up = lax.all_gather(upper, "chan", axis=1, tiled=True)
+    whole_up = jnp.concatenate(
+        lax.all_to_all(jnp.stack([upper] * lax.axis_size("chan")), "chan", 0, 0), axis=1
+    )
     mixed = jnp.dot(whole_low, conv_weight[layer_number, 0], preferred_element_type=jnp.float32)
     mixed = mixed + jnp.dot(whole, conv_weight[layer_number, 1], preferred_element_type=jnp.float32)
     mixed = mixed + jnp.dot(

time: 469 us -> 439 us (0.936)
  waiting for transfers between devices: 395 us -> 343 us
  blocking collectives: 0 us -> 22.4 us
    all_gather x1 -> x0, waiting for transfers between devices: 27.9 us -> none  [shards(): whole_up = lax.all_gather(upper, 'chan', axis=1, tiled=True)]
    all_to_all x0 -> x1, blocking collectives: none -> 22.4 us  [shards(): lax.all_to_all(jnp.stack([upper] * lax.axis_size('chan')), 'chan', 0, 0)]
    all_gather x1, waiting for transfers between devices: 27.4 us -> 6.39 us  [shards(): whole_low = lax.all_gather(lower, 'chan', axis=1, tiled=True)]
    all_gather x1, waiting for transfers between devices: 5.46 us -> 0.01 us  [shards(): whole = lax.all_gather(acted, 'chan', axis=1, tiled=True)]
  transfers between devices with their start and end apart: 12 -> 11, of which waited for: 12 -> 10; matrix products, arithmetic and copies ran while one was open for 6% -> 7% of each run, Pallas kernels for 0% -> 0%
where the time goes in v1:
time: 439 us
  waiting for transfers between devices  343 us (78%)
  matrix products  33.2 us (8%)
  blocking collectives  22.4 us (5%)
  between operations  14.3 us (3%)
  starting transfers between devices  10.6 us (2%)
  other arithmetic  9.47 us (2%)
  local copies, waits for them, and re-layouts  6.07 us (1%)
    reduce_scatter x1, waiting for transfers between devices, shards(): lax.psum_scatter(kernel, 'seq', scatter_dimension=1, tiled=True)  151 us
    all_gather x1, waiting for transfers between devices, shards(): all_blocks = lax.all_gather(block_partial_sums, 'seq', axis=0, tiled=True)  50.6 us
    reduce_scatter x1, waiting for transfers between devices, shards(): lax.psum_scatter(times_t(head_term, head_weight), 'chan', scatter_dimensi...  40.1 us
    reduce_scatter x1, waiting for transfers between devices, shards(): lax.psum_scatter(partial_value, 'chan', scatter_dimension=1, tiled=True)  34.7 us
    all_gather x1, waiting for transfers between devices, shards(): full_state = lax.all_gather(state, 'chan', axis=1, tiled=True)  31.1 us
    ppermute x4, waiting for transfers between devices, shifted(): lax.ppermute(value, axis, [(source, source + steps) for source in range(l...  28.1 us
    all_to_all x1, blocking collectives, shards(): lax.all_to_all(jnp.stack([upper] * lax.axis_size('chan')), 'chan', 0, 0)  22.4 us
    ppermute x4, starting transfers between devices, shifted(): lax.ppermute(value, axis, [(source, source + steps) for source in range(l...  10.2 us
  transfers between devices with their start and end apart: 11, of which 10 were waited for; matrix products, arithmetic and copies ran while one was open for 7% of the time, Pallas kernels for 0%

profile of v1, /device:TPU:2, one launch (start us, length us, event | category | flops | bytes accessed | tf_op | source)
XLA Modules:
  0.0 438.8 jit_solution(9258781175730880586)
XLA Ops:
  7.2 0.0 all-gather.8.cloned.1.call-start
  7.2 2.2 fusion.30
  9.4 0.0 all-gather.8.cloned.1.call-update
  9.4 0.0 all-gather.6.cloned.1.call-start
  9.5 3.8 collective-permute-start
  13.3 8.6 %collective-permute-done = bf16[512,384]{1,0:T(8,128)(2,1)S(1)} collective-permute-done((bf16[512,384]{1,0:T(8,128)(2,1)}, bf16[512,384]{1,0:T(8,128)(2,1)S(1)}, u32[]{:S(2)}, u32[]{:S(2)}) %collective-permute-start) | collective-permute-done | bytes 393248 | tf_op jit(solution)/shard_map/ppermute | solution.py:13
  22.0 0.8 copy-done.8
  22.7 0.0 all-gather.6.cloned.1.call-update
  22.8 0.0 all-gather.10.cloned.1.call-start
  22.8 1.3 collective-permute-start.1
  24.1 11.5 %collective-permute-done.1 = bf16[512,384]{1,0:T(8,128)(2,1)} collective-permute-done((bf16[512,384]{1,0:T(8,128)(2,1)}, bf16[512,384]{1,0:T(8,128)(2,1)}, u32[]{:S(2)}, u32[]{:S(2)}) %collective-permute-start.1) | collective-permute-done | bytes 393248 | tf_op jit(solution)/shard_map/ppermute | solution.py:13
  35.6 1.2 copy.11
  36.8 0.1 stack.22
  36.9 22.4 %all_to_all.5 = bf16[4,512,384]{1,2,0:T(8,128)(2,1)S(1)} all-to-all(bf16[4,512,384]{1,2,0:T(8,128)(2,1)S(1)} %stack.22), channel_id=1, replica_groups=mesh['seq'=64,'chan'=4] {'chan'}, dimensions={0} | all-to-all | bytes 3145728 | tf_op jit(solution)/shard_map/all_to_all | solution.py:52
  59.3 3.2 fusion.6
  62.5 3.7 fusion.10
  66.2 6.4 %all-gather.6.cloned.1.call-done = bf16[512,1536]{1,0:T(8,128)(2,1)} async-done(((bf16[512,384]{1,0:T(8,128)(2,1)}), bf16[512,1536]{1,0:T(8,128)(2,1)}) %all-gather.6.cloned.1.call-update) | async-done | bytes 1572880 | tf_op jit(solution)/shard_map/all_gather | solution.py:50
  72.6 3.9 fusion.3
  76.5 0.0 reduce-scatter.4.cloned.1.call-start
  76.6 31.1 %all-gather.10.cloned.1.call-done = bf16[512,1536]{1,0:T(8,128)(2,1)} async-done(((bf16[512,384]{1,0:T(8,128)(2,1)}), bf16[512,1536]{1,0:T(8,128)(2,1)}) %all-gather.10.cloned.1.call-update) | async-done | bytes 1572880 | tf_op jit(solution)/shard_map/all_gather | solution.py:61
  107.6 5.8 %convert_reduce_fusion = (f32[4,1024]{1,0:T(4,128)}, bf16[512,1024]{1,0:T(8,128)(2,1)}, f32[512,1024]{1,0:T(8,128)S(1)}) fusion(bf16[512,1536]{1,0:T(8,128)(2,1)} %all-gather.10.cloned.1.call-done, bf16[1536,1024]{1,0:T(8,128)(2,1)S(1)} %copy-done), kind=kOutput, calls=%fused_computation.8 | convolution fusion | flops 1615327232 | bytes 7880704 | tf_op jit(solution)/shard_map/dot_general | solution.py:62
  113.5 3.5 fusion.15
  117.0 0.0 all-gather.12.cloned.1.call-start
  117.0 0.5 all-gather.12.cloned.1.call-update
  117.6 0.0 reduce-scatter.6.cloned.1.call-start
  117.6 40.1 %reduce-scatter.4.cloned.1.call-done = f32[512,384]{1,0:T(8,128)} async-done(((f32[512,1536]{1,0:T(8,128)}), f32[512,384]{1,0:T(8,128)}) %reduce-scatter.4.cloned.1.call-update) | async-done | bytes 786448 | tf_op jit(solution)/shard_map/reduce_scatter | solution.py:65
  157.7 1.2 convert_element_type.37
  158.9 3.8 collective-permute-start.3
  162.6 1.3 collective-permute-start.2
  163.9 2.3 fusion.8
  166.2 4.8 %collective-permute-done.3 = bf16[512,384]{1,0:T(8,128)(2,1)S(1)} collective-permute-done((bf16[512,384]{1,0:T(8,128)(2,1)S(1)}, bf16[512,384]{1,0:T(8,128)(2,1)S(1)}, u32[]{:S(2)}, u32[]{:S(2)}) %collective-permute-start.3) | collective-permute-done | bytes 393248 | tf_op jit(solution)/shard_map/ppermute | solution.py:13
  171.0 1.0 fusion.4
  172.0 3.1 collective-permute-done.2
  175.1 0.7 copy-done.4
  175.9 2.7 fusion
  178.6 0.2 reduce-scatter.8.cloned.1.call-start
  178.9 2.6 convolution_bitcast_fusion.1
  181.5 1.0 convolution_bitcast_fusion
  182.6 1.0 convolution_bitcast_fusion.2
  183.6 3.3 pad_maximum_fusion
  186.9 0.7 copy-done.9
  187.6 0.1 convert_reduce_fusion.1
  187.7 50.6 %all-gather.12.cloned.1.call-done = f32[64,4,1024]{2,1,0:T(4,128)} async-done(((f32[1,4,1024]{2,1,0:T(4,128)}), f32[64,4,1024]{2,1,0:T(4,128)}) %all-gather.12.cloned.1.call-update) | async-done | bytes 1048592 | tf_op jit(solution)/shard_map/all_gather | solution.py:89
  238.3 2.6 reshape.30
  240.9 2.4 convolution_multiply_fusion
  243.3 34.7 %reduce-scatter.6.cloned.1.call-done = f32[512,384]{1,0:T(8,128)} async-done(((f32[512,1536]{1,0:T(8,128)}), f32[512,384]{1,0:T(8,128)}) %reduce-scatter.6.cloned.1.call-update) | async-done | bytes 786448 | tf_op jit(solution)/shard_map/reduce_scatter | solution.py:77
  277.9 2.7 fusion.26
  280.7 151.3 %reduce-scatter.8.cloned.1.call-done = f32[3,24,384]{2,1,0:T(8,128)} async-done(((f32[3,1536,384]{2,1,0:T(8,128)}), f32[3,24,384]{2,1,0:T(8,128)}) %reduce-scatter.8.cloned.1.call-update) | async-done | bytes 110608 | tf_op jit(solution)/shard_map/reduce_scatter | solution.py:81
  (26 shorter events, 0.1 us)
Async XLA Ops:
  7.2 100.5 %copy-start = (bf16[1536,1024]{1,0:T(8,128)(2,1)S(1)}, bf16[1536,1024]{1,0:T(8,128)(2,1)}, u32[]{:S(2)}) copy-start(bf16[1536,1024]{1,0:T(8,128)(2,1)} %param.7) | copy-start | bytes 9437188
  7.2 55.3 %all-gather.8.cloned.1.call-start = ((), (), s32[]{:S(2)}) async-start(), calls=%async_computation.5 | async-start | bytes 1966080 | tf_op jit(solution)/shard_map/all_gather | solution.py:49
  9.4 63.1 %all-gather.6.cloned.1.call-start = ((), (), s32[]{:S(2)}) async-start(), calls=%async_computation.4 | async-start | bytes 1966080 | tf_op jit(solution)/shard_map/all_gather | solution.py:50
  9.5 12.5 %collective-permute-start = (bf16[512,384]{1,0:T(8,128)(2,1)}, bf16[512,384]{1,0:T(8,128)(2,1)S(1)}, u32[]{:S(2)}, u32[]{:S(2)}) collective-permute-start(bf16[512,384]{1,0:T(8,128)(2,1)} %fusion.30), channel_id=1, source_target_pairs={{0,8},{4,12},{8,16},{12,20},{16,24},{20,28},{24,32},{28,36},{32,40... | collective-permute-start | bytes 1179656 | tf_op jit(solution)/shard_map/ppermute | solution.py:13
  22.0 0.8 copy-start.8
  22.8 84.9 %all-gather.10.cloned.1.call-start = ((), (), s32[]{:S(2)}) async-start(), calls=%async_computation.6 | async-start | bytes 1966080 | tf_op jit(solution)/shard_map/all_gather | solution.py:61
  22.8 12.8 %collective-permute-start.1 = (bf16[512,384]{1,0:T(8,128)(2,1)}, bf16[512,384]{1,0:T(8,128)(2,1)}, u32[]{:S(2)}, u32[]{:S(2)}) collective-permute-start(bf16[512,384]{1,0:T(8,128)(2,1)} %fusion.30), channel_id=1, source_target_pairs={{8,0},{12,4},{16,8},{20,12},{24,16},{28,20},{32,24},{36,28},{40,32... | collective-permute-start | bytes 1179656 | tf_op jit(solution)/shard_map/ppermute | solution.py:13
  62.5 10.1 %copy-start.2 = (bf16[512,384]{1,0:T(8,128)(2,1)S(1)}, bf16[512,384]{1,0:T(8,128)(2,1)}, u32[]{:S(2)}) copy-start(bf16[512,384]{1,0:T(8,128)(2,1)} %param.5) | copy-start | bytes 1179652
  76.5 81.2 %reduce-scatter.4.cloned.1.call-start = ((), (), s32[]{:S(2)}) async-start(), calls=%async_computation.7 | async-start | bytes 3932160 | tf_op jit(solution)/shard_map/reduce_scatter | solution.py:65
  107.6 5.8 %copy-start.11 = (bf16[512,1024]{1,0:T(8,128)(2,1)S(1)}, bf16[512,1024]{1,0:T(8,128)(2,1)}, u32[]{:S(2)}) copy-start(bf16[512,1024]{1,0:T(8,128)(2,1)} %param.8) | copy-start | bytes 3145732
  117.0 121.3 %all-gather.12.cloned.1.call-start = ((), (), s32[]{:S(2)}) async-start(), calls=%async_computation.10 | async-start | bytes 1064960 | tf_op jit(solution)/shard_map/all_gather | solution.py:89
  117.6 160.4 %reduce-scatter.6.cloned.1.call-start = ((), (), s32[]{:S(2)}) async-start(), calls=%async_computation.8 | async-start | bytes 3932160 | tf_op jit(solution)/shard_map/reduce_scatter | solution.py:77
  158.8 7.4 %copy-start.3 = (bf16[512,384]{1,0:T(8,128)(2,1)}, bf16[512,384]{1,0:T(8,128)(2,1)S(1)}, u32[]{:S(2)}) copy-start(bf16[512,384]{1,0:T(8,128)(2,1)S(1)} %convert_element_type.37) | copy-start | bytes 1179652
  158.8 12.2 %copy-start.1 = (bf16[1,3,1536,384]{3,2,1,0:T(8,128)(2,1)S(1)}, bf16[1,3,1536,384]{3,2,1,0:T(8,128)(2,1)}, u32[]{:S(2)}) copy-start(bf16[1,3,1536,384]{3,2,1,0:T(8,128)(2,1)} %param.6) | copy-start | bytes 10616836
  158.9 12.1 %collective-permute-start.3 = (bf16[512,384]{1,0:T(8,128)(2,1)S(1)}, bf16[512,384]{1,0:T(8,128)(2,1)S(1)}, u32[]{:S(2)}, u32[]{:S(2)}) collective-permute-start(bf16[512,384]{1,0:T(8,128)(2,1)S(1)} %convert_element_type.37), channel_id=1, source_target_pairs={{0,8},{4,12},{8,16},{12,20},{16,24},{20,28},{24,32},{28,36},{32,40... | collective-permute-start | bytes 1179656 | tf_op jit(solution)/shard_map/ppermute | solution.py:13
  162.6 12.5 %collective-permute-start.2 = (bf16[512,384]{1,0:T(8,128)(2,1)S(1)}, bf16[512,384]{1,0:T(8,128)(2,1)S(1)}, u32[]{:S(2)}, u32[]{:S(2)}) collective-permute-start(bf16[512,384]{1,0:T(8,128)(2,1)S(1)} %convert_element_type.37), channel_id=1, source_target_pairs={{8,0},{12,4},{16,8},{20,12},{24,16},{28,20},{32,24},{36,28},{40,32... | collective-permute-start | bytes 1179656 | tf_op jit(solution)/shard_map/ppermute | solution.py:13
  171.0 1.0 copy-start.6
  175.1 0.7 copy-start.4
  178.6 253.3 %reduce-scatter.8.cloned.1.call-start = ((), (), s32[]{:S(2)}) async-start(), calls=%async_computation.9 | async-start | bytes 7188480 | tf_op jit(solution)/shard_map/reduce_scatter | solution.py:81
  178.9 2.7 copy-start.7
  178.9 2.6 copy-start.10
  181.5 1.0 copy-start.5
  186.9 0.7 copy-start.9
Sparse Core Ops, SparseCore 0:
  10.4 31.5 all-gather.7
  43.9 28.6 all-gather.5
  76.6 30.9 all-gather.9
  117.1 40.5 reduce-scatter.3
  160.9 77.3 all-gather.11
  240.7 37.2 reduce-scatter.5
  282.8 149.1 reduce-scatter.7
